TPU v7x, 128 devices: a whole 4x4x4 slice. The times are simulated.
128 devices in a mesh: dp: 16 (over y_hi, x, core), space: 8 (over z, y_lo).
Axes of the slice: x: 4, y: 4 (y_hi: 2, y_lo: 2; y = y_hi * 2 + y_lo), z: 4, core: 2. Of those that a mesh axis runs over, the one named last changes fastest.
Arguments:
- volume: bfloat16 [16, 32, 32, 128], P('dp', 'space'), may hold values from -6 to 6
- first_kernel: bfloat16 [3, 3, 3, 4, 64], replicated, may hold values from -0.625 to 0.625
- mid_kernel: bfloat16 [3, 3, 3, 64, 128], replicated, may hold values from -0.15625 to 0.15625
- deep_kernel: bfloat16 [3, 3, 3, 128, 256], replicated, may hold values from -0.109375 to 0.109375
- deep_cotangent: bfloat16 [16, 16, 16, 16, 256], P('dp', 'space'), may hold values from -6 to 6
Outputs:
- deep_output: bfloat16 [16, 16, 16, 16, 256], P('dp', 'space')
- deep_kernel_grad: float32 [3, 3, 3, 128, 256], P(None, None, None, 'space')
- mid_kernel_grad: float32 [3, 3, 3, 64, 128], replicated
All inputs are finite; a program needn't handle non-finite values.
Results may differ from a plain program's by a relative error of at most 0.024.
Values may be sent and summed in bfloat16 or wider, within the bound.
A program may use at most 128 MiB of HBM per device.

v0:
```python
import math
import jax
import jax.numpy as jnp
from jax import lax
from jax.sharding import PartitionSpec as P

SLOPE = 0.3


def padded_2(block, sides, width):
    for axis, dim in sides:
        count = lax.axis_size(axis)
        forward = [(i, i + 1) for i in range(count - 1)]
        backward = [(target, source) for source, target in forward]
        low = lax.ppermute(
            lax.slice_in_dim(block, block.shape[dim] - width, None, axis=dim), axis, forward
        )
        high = lax.ppermute(lax.slice_in_dim(block, 0, width, axis=dim), axis, backward)
        block = jnp.concatenate([low, block, high], axis=dim)
    return block


def activate(value):
    return SLOPE * value + (1.0 - SLOPE) * value * jax.nn.sigmoid(value)


def activate_slope(value):
    sig = jax.nn.sigmoid(value)
    return SLOPE + (1.0 - SLOPE) * (sig + value * sig * (1.0 - sig))


def conv_depth(padded, kernel):
    return lax.conv_general_dilated(
        padded[None],
        kernel,
        (1, 1, 1),
        [(0, 0), (1, 1), (1, 1)],
        dimension_numbers=("NDHWC", "DHWIO", "NDHWC"),
        preferred_element_type=jnp.float32,
    )[0]


def pool_cells(values):
    dd, hh, ww, cc = values.shape
    return values.reshape(dd // 2, 2, hh // 2, 2, ww // 2, 2, cc).mean(axis=(1, 3, 5))


def expand(values):
    return jnp.repeat(jnp.repeat(jnp.repeat(values, 2, 0), 2, 1), 2, 2)


def kernel_grad(padded, cotangent):
    dd, hh, ww, _ = cotangent.shape
    tap_list = []
    for depth_off in range(3):
        for row_off in range(3):
            for col_off in range(3):
                window = padded[
                    depth_off : depth_off + dd, row_off : row_off + hh, col_off : col_off + ww
                ]
                tap_list.append(
                    jnp.einsum(
                        "dhwi,dhwo->io", window, cotangent, preferred_element_type=jnp.float32
                    )
                )
    return jnp.stack(tap_list).reshape(3, 3, 3, padded.shape[-1], cotangent.shape[-1])


def pad_sides(values):
    return jnp.pad(values, ((0, 0), (1, 1), (1, 1), (0, 0)))


def pad_depth(values):
    return jnp.pad(values, ((1, 1), (0, 0), (0, 0), (0, 0)))


def pad_cells(values):
    return jnp.pad(values, ((1, 1), (1, 1), (1, 1), (0, 0)))


def on_device(volume, first_kernel, mid_kernel, deep_kernel, deep_cotangent):
    slab_depth = volume.shape[1]
    side_cells = volume.shape[2]
    in_channels = volume.shape[3] // side_cells
    space_count = lax.axis_size("space")
    space_index = lax.axis_index("space")
    input_field = volume[0].reshape(slab_depth, side_cells, side_cells, in_channels)
    padded = padded_2(input_field, (("space", 0),), 1)
    own_hidden = activate(conv_depth(padded, first_kernel)).astype(jnp.bfloat16)
    hidden = padded_2(own_hidden, (("space", 0),), 1)
    pre_mid = conv_depth(hidden, mid_kernel)
    pooled = pool_cells(activate(pre_mid)).astype(jnp.bfloat16)
    cotangent = deep_cotangent[0].astype(jnp.float32)
    columns = lax.all_to_all(pooled, "space", split_axis=3, concat_axis=0, tiled=True)
    chan_width = columns.shape[3]
    chan_start = space_index * chan_width
    kernel_part = lax.dynamic_slice_in_dim(deep_kernel, chan_start, chan_width, 3)
    partial_value = conv_depth(pad_depth(columns), kernel_part)
    pre_deep = lax.psum_scatter(partial_value, "space", scatter_dimension=0, tiled=True)
    grad_pre = (cotangent * activate_slope(pre_deep)).astype(jnp.bfloat16)
    all_cotangent = lax.all_gather(grad_pre, "space", axis=0, tiled=True)
    deep_grad = kernel_grad(pad_cells(columns), all_cotangent)
    flipped_part = jnp.swapaxes(kernel_part[::-1, ::-1, ::-1], 3, 4)
    back_grad = conv_depth(pad_depth(all_cotangent), flipped_part).astype(jnp.bfloat16)
    pooled_grad = lax.all_to_all(back_grad, "space", split_axis=0, concat_axis=3, tiled=True)
    deep_grad = lax.psum(deep_grad.astype(jnp.bfloat16), "dp").astype(jnp.float32)
    grad_mid = (expand(pooled_grad.astype(jnp.float32)) * 0.125 * activate_slope(pre_mid)).astype(
        jnp.bfloat16
    )
    mid_grad = lax.psum(kernel_grad(pad_sides(hidden), grad_mid), ("dp", "space"))
    device_total = lax.axis_size("dp") * space_count
    cell_count = slab_depth * side_cells * side_cells
    deep_scale = math.sqrt(device_total * cell_count // 8)
    mid_scale = math.sqrt(device_total * cell_count)
    deep_output = activate(pre_deep).astype(jnp.bfloat16)[None]
    return (deep_output, deep_grad / deep_scale, mid_grad / mid_scale)


def solution(mesh):
    in_specs = (P("dp", "space", None, None), P(), P(), P(), P("dp", "space", None, None, None))
    out_specs = (P("dp", "space", None, None, None), P(None, None, None, "space", None), P())
    return jax.shard_map(
        on_device, mesh=mesh, in_specs=in_specs, out_specs=out_specs, check_vma=False
    )
```

profile of v0, /device:TPU:1, one launch (start us, length us, event | category | flops | bytes accessed | tf_op | source)
XLA Modules:
  0.0 628.2 jit_solution(16983838333227108347)
XLA Ops:
  8.2 4.0 collective-permute-start
  13.6 3.4 collective-permute-done.1
  18.2 7.4 %add_convert_fusion = (bf16[4,32,8,5,64]{4,2,3,1,0:T(8,128)(2,1)}, f32[4,32,8,5,64]{4,2,3,1,0:T(8,128)S(1)}, f32[4,32,8,5,64]{4,2,3,1,0:T(8,128)S(1)}, f32[4,32,8,5,64]{4,2,3,1,0:T(8,128)S(1)}) fusion(pred[8,5]{0,1:T(8,128)(4,1)S(1)} %copy-done.21, bf16[3,3,3,4,64]{4,3,2,1,0:T(4,128)(2,1)S(1)} %copy-done.20, bf16[6,32,1,7,2,4]{3,5,4,1,0,2:T(4,128)(2,1)S(1)} %slice.257, ...), kind=kOutput, calls=%fused_computation.31 | convolution fusion | flops 72511488 | bytes 4684328 | tf_op jit(solution)/shard_map/conv_general_dilated | solution.py:33
  27.5 4.8 fusion.30
  32.4 4.3 collective-permute-start.2
  38.0 2.0 collective-permute-done.2
  40.0 7.1 %collective-permute-done.3 = bf16[1,32,32,64]{3,2,1,0:T(8,128)(2,1)S(1)} collective-permute-done((bf16[1,32,32,64]{3,2,1,0:T(8,128)(2,1)S(1)}, bf16[1,32,32,64]{3,2,1,0:T(8,128)(2,1)S(1)}, u32[]{:S(2)}, u32[]{:S(2)}) %collective-permute-start.3) | collective-permute-done | bytes 131104 | tf_op jit(solution)/shard_map/ppermute | solution.py:18
  50.6 6.6 %broadcast_multiply_fusion.1 = (f32[4,32,8,5,128]{4,2,3,1,0:T(8,128)S(1)}, f32[4,32,8,5,128]{4,2,3,1,0:T(8,128)S(1)}, f32[4,32,8,5,128]{4,2,3,1,0:T(8,128)S(1)}, f32[4,32,8,5,128]{4,2,3,1,0:T(8,128)}) fusion(bf16[3,3,3,64,128]{4,3,2,1,0:T(8,128)(2,1)S(1)} %copy-done.19, bf16[6,32,1,7,2,64]{5,3,4,1,0,2:T(8,128)(2,1)S(1)} %slice.263, ...), kind=kOutput, calls=%fused_computation.97 | convolution fusion | flops 2225799168 | bytes 12255272 | tf_op jit(solution)/shard_map/conv_general_dilated | solution.py:33
  58.6 2.1 fusion.28
  60.7 2.9 reduce_sum.9
  67.0 5.2 all-to-all-start
  72.3 5.5 all-to-all-done
  82.5 4.0 copy.321
  86.4 2.8 pad.24.clone
  89.3 5.7 copy.215
  96.8 4.5 broadcast_select_fusion
  101.3 2.0 copy.216
  103.3 2.4 slice_bitcast_fusion
  106.2 93.6 %reduce-scatter.2.cloned.1.call-done = f32[2,16,16,256]{3,1,2,0:T(8,128)} async-done(((f32[16,16,16,256]{3,1,2,0:T(8,128)}), f32[2,16,16,256]{3,1,2,0:T(8,128)}) %reduce-scatter.2.cloned.1.call-update) | async-done | bytes 524304 | tf_op jit(solution)/shard_map/reduce_scatter | solution.py:99
  208.3 46.0 %all-gather.2.cloned.1.call-done = bf16[16,16,16,256]{3,2,1,0:T(8,128)(2,1)} async-done(((bf16[2,16,16,256]{3,2,1,0:T(8,128)(2,1)}), bf16[16,16,16,256]{3,2,1,0:T(8,128)(2,1)}) %all-gather.2.cloned.1.call-update) | async-done | bytes 2097168 | tf_op jit(solution)/shard_map/all_gather | solution.py:101
  254.3 2.5 copy.219
  259.6 22.7 %select_convert_fusion = bf16[16,16,8,3,16]{4,2,3,1,0:T(8,128)(2,1)S(1)} fusion(pred[8,3]{0,1:T(4,128)(4,1)S(1)} %copy-done.22, bf16[18,16,1,7,2,256]{5,3,4,1,0,2:T(8,128)(2,1)S(1)} %slice.269, bf16[18,16,1,8,3,256]{5,3,4,1,0,2:T(8,128)(2,1)S(1)} %copy.221, bf16[3,3,3,128,256]{4,3,2,1,0:T(8,128)(2,1)S(1)} %copy-done, s32[]{:T(128)S(6)} %select_n.3), kind=kOutput, calls=%fused_computation.13 | convolution fusion | flops 1320222720 | bytes 6316548 | tf_op jit(solution)/shard_map/conv_general_dilated | solution.py:33
  283.9 3.1 reshape.225
  287.0 3.4 all-to-all-start.1
  290.6 3.0 fusion.179
  293.5 2.9 fusion.177
  332.1 2.6 copy.314
  334.7 2.6 reshape.222
  365.0 101.8 %all-reduce.7.cloned.1.call-done = bf16[3,3,3,16,256]{4,3,2,1,0:T(8,128)(2,1)} async-done(((bf16[3,3,3,16,256]{4,3,2,1,0:T(8,128)(2,1)}), bf16[3,3,3,16,256]{4,3,2,1,0:T(8,128)(2,1)}) %all-reduce.7.cloned.1.call-update) | async-done | bytes 221200 | tf_op jit(solution)/shard_map/psum | solution.py:106
  466.9 1.7 convert_multiply_fusion.2
  468.6 150.7 %all-reduce.9.cloned.1.call-done = f32[3,3,3,64,128]{4,3,2,1,0:T(8,128)} async-done(((f32[3,3,3,64,128]{4,3,2,1,0:T(8,128)}), f32[3,3,3,64,128]{4,3,2,1,0:T(8,128)}) %all-reduce.9.cloned.1.call-update) | async-done | bytes 884752 | tf_op jit(solution)/shard_map/psum | solution.py:110
  619.3 2.2 broadcast_multiply_fusion.2
  (159 shorter events, 98.2 us)
Async XLA Ops:
  7.2 89.5 %copy-start = (bf16[3,3,3,128,256]{4,3,2,1,0:T(8,128)(2,1)S(1)}, bf16[3,3,3,128,256]{4,3,2,1,0:T(8,128)(2,1)}, u32[]{:S(2)}) copy-start(bf16[3,3,3,128,256]{4,3,2,1,0:T(8,128)(2,1)} %param.8) | copy-start | bytes 5308420
  7.2 11.0 %copy-start.21 = (pred[8,5]{0,1:T(8,128)(4,1)S(1)}, pred[8,5]{0,1:T(8,128)(4,1)}, u32[]{:S(2)}) copy-start(pred[8,5]{0,1:T(8,128)(4,1)} %constant.63) | copy-start | bytes 124
  7.2 11.0 %copy-start.20 = (bf16[3,3,3,4,64]{4,3,2,1,0:T(4,128)(2,1)S(1)}, bf16[3,3,3,4,64]{4,3,2,1,0:T(4,128)(2,1)}, u32[]{:S(2)}) copy-start(bf16[3,3,3,4,64]{4,3,2,1,0:T(4,128)(2,1)} %param.6) | copy-start | bytes 41476
  8.2 5.3 collective-permute-start
  12.3 4.7 collective-permute-start.1
  32.3 16.2 %copy-start.6 = (bf16[4,32,1,32,64]{4,3,1,2,0:T(8,128)(2,1)}, bf16[4,32,1,32,64]{4,3,1,2,0:T(8,128)(2,1)S(1)}, u32[]{:S(2)}) copy-start(bf16[4,32,1,32,64]{4,3,1,2,0:T(8,128)(2,1)S(1)} %fusion.30) | copy-start | bytes 1572868
  32.4 7.6 %collective-permute-start.2 = (bf16[1,32,32,64]{3,2,1,0:T(8,128)(2,1)S(1)}, bf16[1,32,32,64]{3,2,1,0:T(8,128)(2,1)S(1)}, u32[]{:S(2)}, u32[]{:S(2)}) collective-permute-start(bf16[1,32,32,64]{3,2,1,0:T(8,128)(2,1)S(1)} %get-tuple-element.18), channel_id=1, source_target_pairs={{0,1},{1,2},{2,3},{3,4},{4,5},{5,6},{6,7},{8,9},{9,10},{10,11},{11... | collective-permute-start | bytes 393224 | tf_op jit(solution)/shard_map/ppermute | solution.py:15
  36.7 10.3 %collective-permute-start.3 = (bf16[1,32,32,64]{3,2,1,0:T(8,128)(2,1)S(1)}, bf16[1,32,32,64]{3,2,1,0:T(8,128)(2,1)S(1)}, u32[]{:S(2)}, u32[]{:S(2)}) collective-permute-start(bf16[1,32,32,64]{3,2,1,0:T(8,128)(2,1)S(1)} %get-tuple-element.19), channel_id=1, source_target_pairs={{1,0},{2,1},{3,2},{4,3},{5,4},{6,5},{7,6},{9,8},{10,9},{11,10},{12... | collective-permute-start | bytes 393224 | tf_op jit(solution)/shard_map/ppermute | solution.py:18
  40.0 8.6 %copy-start.16 = (bf16[1,32,32,64]{3,2,1,0:T(8,128)(2,1)}, bf16[1,32,32,64]{3,2,1,0:T(8,128)(2,1)S(1)}, u32[]{:S(2)}) copy-start(bf16[1,32,32,64]{3,2,1,0:T(8,128)(2,1)S(1)} %collective-permute-done.2) | copy-start | bytes 393220
  47.0 1.5 copy-start.14
  49.6 1.0 copy-start.19
  67.0 10.8 %all-to-all-start = ((bf16[8,2,4096]{2,1,0:T(2,128)(2,1)}), bf16[8,2,4096]{2,1,0:T(2,128)(2,1)S(1)}, u32[]{:S(2)}, u32[]{:S(2)}) async-start(bf16[8,2,4096]{2,1,0:T(2,128)(2,1)} %reshape.223), calls=%async_computation | async-start | bytes 262144 | tf_op jit(solution)/shard_map/all_to_all | solution.py:94
  72.3 127.6 %reduce-scatter.2.cloned.1.call-start = ((), (), s32[]{:S(2)}) async-start(), calls=%async_computation.3 | async-start | bytes 4718592 | tf_op jit(solution)/shard_map/reduce_scatter | solution.py:99
  89.3 7.4 %copy-start.22 = (pred[8,3]{0,1:T(4,128)(4,1)S(1)}, pred[8,3]{0,1:T(4,128)(4,1)}, u32[]{:S(2)}) copy-start(pred[8,3]{0,1:T(4,128)(4,1)} %constant.62) | copy-start | bytes 76
  94.9 1.8 copy-start.8
  105.7 94.1 %copy-start.13 = (bf16[1,2,16,16,256]{4,3,2,1,0:T(8,128)(2,1)S(1)}, bf16[1,2,16,16,256]{4,3,2,1,0:T(8,128)(2,1)}, u32[]{:S(2)}) copy-start(bf16[1,2,16,16,256]{4,3,2,1,0:T(8,128)(2,1)} %param.9) | copy-start | bytes 786436
  105.8 148.5 %all-gather.2.cloned.1.call-start = ((), (), s32[]{:S(2)}) async-start(), calls=%async_computation.4 | async-start | bytes 2359296 | tf_op jit(solution)/shard_map/all_gather | solution.py:101
  202.0 2.8 copy-start.9
  205.3 1.5 copy-start.3
  287.0 44.2 %all-to-all-start.1 = ((bf16[8,2,4096]{2,1,0:T(2,128)(2,1)}), bf16[8,2,4096]{2,1,0:T(2,128)(2,1)S(1)}, u32[]{:S(2)}, u32[]{:S(2)}) async-start(bf16[8,2,4096]{2,1,0:T(2,128)(2,1)} %reshape.225), calls=%async_computation.2 | async-start | bytes 262144 | tf_op jit(solution)/shard_map/all_to_all | solution.py:105
  290.4 176.5 %all-reduce.7.cloned.1.call-start = ((), (), s32[]{:S(2)}) async-start(), calls=%async_computation.5 | async-start | bytes 442368 | tf_op jit(solution)/shard_map/psum | solution.py:106
  293.5 2.9 copy-start.2
  331.1 288.2 %all-reduce.9.cloned.1.call-start = ((), (), s32[]{:S(2)}) async-start(), calls=%async_computation.6 | async-start | bytes 1769472 | tf_op jit(solution)/shard_map/psum | solution.py:110
  337.2 1.6 copy-start.5
  340.6 1.8 copy-start.4
  342.3 1.4 copy-start.10
  345.7 1.2 copy-start.7
  345.7 1.3 copy-start.17
  352.4 1.2 copy-start.11
  359.0 1.0 copy-start.15
  362.6 258.9 %copy-start.1 = (bf16[3,3,3,128,256]{4,3,2,1,0:T(8,128)(2,1)S(1)}, bf16[3,3,3,128,256]{4,3,2,1,0:T(8,128)(2,1)}, u32[]{:S(2)}) copy-start(bf16[3,3,3,128,256]{4,3,2,1,0:T(8,128)(2,1)} %param.8) | copy-start | bytes 5308420
  363.3 0.9 copy-start.12
  (1 other events, 0.7 us)
Sparse Core Ops, SparseCore 0:
  105.9 93.9 reduce-scatter.1
  202.2 52.0 all-gather.1
  331.2 135.5 all-reduce.6
  472.8 146.4 all-reduce.8
where the time goes:
time: 638 us; the launch traced here: 628 us
  waiting for transfers between devices  410 us (64%)
  matrix products  99 us (16%)
  local copies, waits for them, and re-layouts  65.3 us (10%)
  starting transfers between devices  20.2 us (3%)
  other arithmetic  18.8 us (3%)
  between operations  14.7 us (2%)
    psum x1, waiting for transfers between devices, on_device(): lax.psum(kernel_grad(pad_sides(hidden), grad_mid), ('dp', 'space'))  151 us
    psum x1, waiting for transfers between devices, on_device(): lax.psum(deep_grad.astype(jnp.bfloat16), 'dp').astype(jnp.float32)  102 us
    reduce_scatter x1, waiting for transfers between devices, on_device(): lax.psum_scatter(partial_value, 'space', scatter_dimension=0, tiled=True)  93.6 us
    dot_general x54, matrix products, kernel_grad(): jnp.einsum('dhwi,dhwo->io', window, cotangent, preferred_element_type=jnp...  57.9 us
    all_gather x1, waiting for transfers between devices, on_device(): all_cotangent = lax.all_gather(grad_pre, 'space', axis=0, tiled=True)  46 us
    conv_general_dilated x4, matrix products, conv_depth(): lax.conv_general_dilated(padded[None], kernel, (1, 1, 1), [(0, 0), (1, 1)...  41.1 us
    unnamed x55, local copies, waits for them, and re-layouts  22.3 us
    conv_general_dilated x11, local copies, waits for them, and re-layouts, conv_depth(): lax.conv_general_dilated(padded[None], kernel, (1, 1, 1), [(0, 0), (1, 1)...  15.4 us
  transfers between devices with their start and end apart: 10, of which 8 were waited for; matrix products, arithmetic and copies ran while one was open for 12% of the time, Pallas kernels for 0%

commit v1 on v0

--- a/solution.py
+++ b/solution.py
@@ -103,7 +103,9 @@
     flipped_part = jnp.swapaxes(kernel_part[::-1, ::-1, ::-1], 3, 4)
     back_grad = conv_depth(pad_depth(all_cotangent), flipped_part).astype(jnp.bfloat16)
     pooled_grad = lax.all_to_all(back_grad, "space", split_axis=0, concat_axis=3, tiled=True)
-    deep_grad = lax.psum(deep_grad.astype(jnp.bfloat16), "dp").astype(jnp.float32)
+    deep_grad = jnp.sum(lax.all_gather(deep_grad.astype(jnp.bfloat16), "dp"), axis=0).astype(
+        jnp.float32
+    )
     grad_mid = (expand(pooled_grad.astype(jnp.float32)) * 0.125 * activate_slope(pre_mid)).astype(
         jnp.bfloat16
     )

time: 638 us -> 594 us (0.931)
  waiting for transfers between devices: 410 us -> 352 us
  other arithmetic: 18.8 us -> 29.5 us
    psum x1 -> x0, waiting for transfers between devices: 102 us -> none  [on_device(): lax.psum(deep_grad.astype(jnp.bfloat16), 'dp').astype(jnp.float32)]
    all_gather x0 -> x1, waiting for transfers between devices: none -> 53.5 us  [on_device(): lax.all_gather(deep_grad.astype(jnp.bfloat16), 'dp')]
    psum x1, waiting for transfers between devices: 151 us -> 141 us  [on_device(): lax.psum(kernel_grad(pad_sides(hidden), grad_mid), ('dp', 'space'))]
    convert_element_type x1, other arithmetic: 4.8 us -> 13.7 us  [on_device(): own_hidden = activate(conv_depth(padded, first_kernel)).astype(jnp.bfloat16)]
  transfers between devices with their start and end apart: 10 -> 10, of which waited for: 8 -> 8; matrix products, arithmetic and copies ran while one was open for 12% -> 9% of each run, Pallas kernels for 0% -> 0%
where the time goes in v1:
time: 594 us; the launch traced here: 584 us
  waiting for transfers between devices  352 us (59%)
  matrix products  102 us (17%)
  local copies, waits for them, and re-layouts  65.3 us (11%)
  other arithmetic  29.5 us (5%)
  starting transfers between devices  20 us (3%)
  between operations  14.7 us (2%)
    psum x1, waiting for transfers between devices, on_device(): lax.psum(kernel_grad(pad_sides(hidden), grad_mid), ('dp', 'space'))  141 us
    reduce_scatter x1, waiting for transfers between devices, on_device(): lax.psum_scatter(partial_value, 'space', scatter_dimension=0, tiled=True)  93.9 us
    dot_general x54, matrix products, kernel_grad(): jnp.einsum('dhwi,dhwo->io', window, cotangent, preferred_element_type=jnp...  61.3 us
    all_gather x1, waiting for transfers between devices, on_device(): lax.all_gather(deep_grad.astype(jnp.bfloat16), 'dp')  53.5 us
    all_gather x1, waiting for transfers between devices, on_device(): all_cotangent = lax.all_gather(grad_pre, 'space', axis=0, tiled=True)  46 us
    conv_general_dilated x4, matrix products, conv_depth(): lax.conv_general_dilated(padded[None], kernel, (1, 1, 1), [(0, 0), (1, 1)...  41.1 us
    unnamed x55, local copies, waits for them, and re-layouts  22.3 us
    conv_general_dilated x11, local copies, waits for them, and re-layouts, conv_depth(): lax.conv_general_dilated(padded[None], kernel, (1, 1, 1), [(0, 0), (1, 1)...  15.4 us
  transfers between devices with their start and end apart: 10, of which 8 were waited for; matrix products, arithmetic and copies ran while one was open for 9% of the time, Pallas kernels for 0%

profile of v1, /device:TPU:1, one launch (start us, length us, event | category | flops | bytes accessed | tf_op | source)
XLA Modules:
  0.0 584.3 jit_solution(4557847056751175654)
XLA Ops:
  8.2 4.0 collective-permute-start
  13.6 3.4 collective-permute-done.1
  18.2 7.4 %add_convert_fusion = (bf16[4,32,8,5,64]{4,2,3,1,0:T(8,128)(2,1)}, f32[4,32,8,5,64]{4,2,3,1,0:T(8,128)S(1)}, f32[4,32,8,5,64]{4,2,3,1,0:T(8,128)S(1)}, f32[4,32,8,5,64]{4,2,3,1,0:T(8,128)S(1)}) fusion(pred[8,5]{0,1:T(8,128)(4,1)S(1)} %copy-done.21, bf16[3,3,3,4,64]{4,3,2,1,0:T(4,128)(2,1)S(1)} %copy-done.20, bf16[6,32,1,7,2,4]{3,5,4,1,0,2:T(4,128)(2,1)S(1)} %slice.257, ...), kind=kOutput, calls=%fused_computation.31 | convolution fusion | flops 72511488 | bytes 4684328 | tf_op jit(solution)/shard_map/conv_general_dilated | solution.py:33
  27.5 13.7 %fusion.30 = bf16[4,32,1,32,64]{4,3,1,2,0:T(8,128)(2,1)S(1)} fusion(f32[4,32,1,32,64]{4,1,3,0,2:T(8,128)S(1)} %slice.260, f32[4,32,1,32,64]{4,1,3,0,2:T(8,128)S(1)} %slice.259, f32[4,32,1,32,64]{4,1,3,0,2:T(8,128)S(1)} %slice.258), kind=kLoop, calls=%fused_computation.64 | loop fusion | flops 786432 | bytes 3670016 | tf_op jit(solution)/shard_map/convert_element_type | solution.py:89
  41.3 4.3 collective-permute-start.2
  48.9 7.1 %collective-permute-done.3 = bf16[1,32,32,64]{3,2,1,0:T(8,128)(2,1)S(1)} collective-permute-done((bf16[1,32,32,64]{3,2,1,0:T(8,128)(2,1)S(1)}, bf16[1,32,32,64]{3,2,1,0:T(8,128)(2,1)S(1)}, u32[]{:S(2)}, u32[]{:S(2)}) %collective-permute-start.3) | collective-permute-done | bytes 131104 | tf_op jit(solution)/shard_map/ppermute | solution.py:18
  59.5 6.6 %broadcast_multiply_fusion.1 = (f32[4,32,8,5,128]{4,2,3,1,0:T(8,128)S(1)}, f32[4,32,8,5,128]{4,2,3,1,0:T(8,128)S(1)}, f32[4,32,8,5,128]{4,2,3,1,0:T(8,128)S(1)}, f32[4,32,8,5,128]{4,2,3,1,0:T(8,128)}) fusion(bf16[3,3,3,64,128]{4,3,2,1,0:T(8,128)(2,1)S(1)} %copy-done.19, bf16[6,32,1,7,2,64]{5,3,4,1,0,2:T(8,128)(2,1)S(1)} %slice.263, ...), kind=kOutput, calls=%fused_computation.97 | convolution fusion | flops 2225799168 | bytes 12255272 | tf_op jit(solution)/shard_map/conv_general_dilated | solution.py:33
  67.5 2.1 fusion.28
  69.6 2.9 reduce_sum.21
  76.2 5.2 all-to-all-start
  81.4 5.5 all-to-all-done
  91.6 4.0 copy.321
  95.6 2.8 pad.24.clone
  98.4 5.7 copy.215
  105.9 4.5 broadcast_select_fusion
  112.4 2.4 slice_bitcast_fusion
  115.1 93.9 %reduce-scatter.2.cloned.1.call-done = f32[2,16,16,256]{3,1,2,0:T(8,128)} async-done(((f32[16,16,16,256]{3,1,2,0:T(8,128)}), f32[2,16,16,256]{3,1,2,0:T(8,128)}) %reduce-scatter.2.cloned.1.call-update) | async-done | bytes 524304 | tf_op jit(solution)/shard_map/reduce_scatter | solution.py:99
  217.5 46.0 %all-gather.3.cloned.1.call-done = bf16[16,16,16,256]{3,2,1,0:T(8,128)(2,1)} async-done(((bf16[2,16,16,256]{3,2,1,0:T(8,128)(2,1)}), bf16[16,16,16,256]{3,2,1,0:T(8,128)(2,1)}) %all-gather.3.cloned.1.call-update) | async-done | bytes 2097168 | tf_op jit(solution)/shard_map/all_gather | solution.py:101
  263.4 2.5 copy.219
  268.7 22.7 %select_convert_fusion = bf16[16,16,8,3,16]{4,2,3,1,0:T(8,128)(2,1)S(1)} fusion(pred[8,3]{0,1:T(4,128)(4,1)S(1)} %copy-done.22, bf16[18,16,1,7,2,256]{5,3,4,1,0,2:T(8,128)(2,1)S(1)} %slice.269, bf16[18,16,1,8,3,256]{5,3,4,1,0,2:T(8,128)(2,1)S(1)} %copy.221, bf16[3,3,3,128,256]{4,3,2,1,0:T(8,128)(2,1)S(1)} %copy-done, s32[]{:T(128)S(6)} %select_n.3), kind=kOutput, calls=%fused_computation.13 | convolution fusion | flops 1320222720 | bytes 6316548 | tf_op jit(solution)/shard_map/conv_general_dilated | solution.py:33
  293.0 3.1 reshape.235
  296.1 3.4 all-to-all-start.1
  299.8 3.0 fusion.179
  302.7 2.9 fusion.177
  338.0 2.6 copy.314
  340.6 2.3 reshape.232
  370.1 2.8 fusion.129
  372.9 3.0 fusion.127
  377.4 140.9 %all-reduce.6.cloned.1.call-done = f32[3,3,3,64,128]{4,3,2,1,0:T(8,128)} async-done(((f32[3,3,3,64,128]{4,3,2,1,0:T(8,128)}), f32[3,3,3,64,128]{4,3,2,1,0:T(8,128)}) %all-reduce.6.cloned.1.call-update) | async-done | bytes 884752 | tf_op jit(solution)/shard_map/psum | solution.py:112
  518.3 2.3 broadcast_multiply_fusion.2
  520.6 53.5 %all-gather.5.cloned.1.call-done = bf16[16,3,3,3,16,256]{5,4,3,2,1,0:T(8,128)(2,1)} async-done(((bf16[1,3,3,3,16,256]{5,4,3,2,1,0:T(8,128)(2,1)}), bf16[16,3,3,3,16,256]{5,4,3,2,1,0:T(8,128)(2,1)}) %all-gather.5.cloned.1.call-update) | async-done | bytes 3538960 | tf_op jit(solution)/shard_map/all_gather | solution.py:106
  574.1 2.6 reduce_sum.22
  (160 shorter events, 100.6 us)
Async XLA Ops:
  7.2 98.6 %copy-start = (bf16[3,3,3,128,256]{4,3,2,1,0:T(8,128)(2,1)S(1)}, bf16[3,3,3,128,256]{4,3,2,1,0:T(8,128)(2,1)}, u32[]{:S(2)}) copy-start(bf16[3,3,3,128,256]{4,3,2,1,0:T(8,128)(2,1)} %param.8) | copy-start | bytes 5308420
  7.2 11.0 %copy-start.21 = (pred[8,5]{0,1:T(8,128)(4,1)S(1)}, pred[8,5]{0,1:T(8,128)(4,1)}, u32[]{:S(2)}) copy-start(pred[8,5]{0,1:T(8,128)(4,1)} %constant.64) | copy-start | bytes 124
  7.2 11.0 %copy-start.20 = (bf16[3,3,3,4,64]{4,3,2,1,0:T(4,128)(2,1)S(1)}, bf16[3,3,3,4,64]{4,3,2,1,0:T(4,128)(2,1)}, u32[]{:S(2)}) copy-start(bf16[3,3,3,4,64]{4,3,2,1,0:T(4,128)(2,1)} %param.6) | copy-start | bytes 41476
  8.2 5.3 collective-permute-start
  12.3 4.7 collective-permute-start.1
  41.3 16.2 %copy-start.6 = (bf16[4,32,1,32,64]{4,3,1,2,0:T(8,128)(2,1)}, bf16[4,32,1,32,64]{4,3,1,2,0:T(8,128)(2,1)S(1)}, u32[]{:S(2)}) copy-start(bf16[4,32,1,32,64]{4,3,1,2,0:T(8,128)(2,1)S(1)} %fusion.30) | copy-start | bytes 1572868
  41.3 7.6 %collective-permute-start.2 = (bf16[1,32,32,64]{3,2,1,0:T(8,128)(2,1)S(1)}, bf16[1,32,32,64]{3,2,1,0:T(8,128)(2,1)S(1)}, u32[]{:S(2)}, u32[]{:S(2)}) collective-permute-start(bf16[1,32,32,64]{3,2,1,0:T(8,128)(2,1)S(1)} %get-tuple-element.18), channel_id=1, source_target_pairs={{0,1},{1,2},{2,3},{3,4},{4,5},{5,6},{6,7},{8,9},{9,10},{10,11},{11... | collective-permute-start | bytes 393224 | tf_op jit(solution)/shard_map/ppermute | solution.py:15
  45.6 10.3 %collective-permute-start.3 = (bf16[1,32,32,64]{3,2,1,0:T(8,128)(2,1)S(1)}, bf16[1,32,32,64]{3,2,1,0:T(8,128)(2,1)S(1)}, u32[]{:S(2)}, u32[]{:S(2)}) collective-permute-start(bf16[1,32,32,64]{3,2,1,0:T(8,128)(2,1)S(1)} %get-tuple-element.19), channel_id=1, source_target_pairs={{1,0},{2,1},{3,2},{4,3},{5,4},{6,5},{7,6},{9,8},{10,9},{11,10},{12... | collective-permute-start | bytes 393224 | tf_op jit(solution)/shard_map/ppermute | solution.py:18
  48.9 8.6 %copy-start.16 = (bf16[1,32,32,64]{3,2,1,0:T(8,128)(2,1)}, bf16[1,32,32,64]{3,2,1,0:T(8,128)(2,1)S(1)}, u32[]{:S(2)}) copy-start(bf16[1,32,32,64]{3,2,1,0:T(8,128)(2,1)S(1)} %collective-permute-done.2) | copy-start | bytes 393220
  55.9 1.5 copy-start.14
  58.5 1.0 copy-start.19
  76.2 10.8 %all-to-all-start = ((bf16[8,2,4096]{2,1,0:T(2,128)(2,1)}), bf16[8,2,4096]{2,1,0:T(2,128)(2,1)S(1)}, u32[]{:S(2)}, u32[]{:S(2)}) async-start(bf16[8,2,4096]{2,1,0:T(2,128)(2,1)} %reshape.233), calls=%async_computation | async-start | bytes 262144 | tf_op jit(solution)/shard_map/all_to_all | solution.py:94
  81.4 127.6 %reduce-scatter.2.cloned.1.call-start = ((), (), s32[]{:S(2)}) async-start(), calls=%async_computation.3 | async-start | bytes 4718592 | tf_op jit(solution)/shard_map/reduce_scatter | solution.py:99
  98.4 7.4 %copy-start.22 = (pred[8,3]{0,1:T(4,128)(4,1)S(1)}, pred[8,3]{0,1:T(4,128)(4,1)}, u32[]{:S(2)}) copy-start(pred[8,3]{0,1:T(4,128)(4,1)} %constant.63) | copy-start | bytes 76
  104.1 1.8 copy-start.8
  114.9 94.1 %copy-start.13 = (bf16[1,2,16,16,256]{4,3,2,1,0:T(8,128)(2,1)S(1)}, bf16[1,2,16,16,256]{4,3,2,1,0:T(8,128)(2,1)}, u32[]{:S(2)}) copy-start(bf16[1,2,16,16,256]{4,3,2,1,0:T(8,128)(2,1)} %param.9) | copy-start | bytes 786436
  114.9 148.5 %all-gather.3.cloned.1.call-start = ((), (), s32[]{:S(2)}) async-start(), calls=%async_computation.4 | async-start | bytes 2359296 | tf_op jit(solution)/shard_map/all_gather | solution.py:101
  211.2 2.8 copy-start.9
  214.5 1.5 copy-start.3
  296.1 41.0 %all-to-all-start.1 = ((bf16[8,2,4096]{2,1,0:T(2,128)(2,1)}), bf16[8,2,4096]{2,1,0:T(2,128)(2,1)S(1)}, u32[]{:S(2)}, u32[]{:S(2)}) async-start(bf16[8,2,4096]{2,1,0:T(2,128)(2,1)} %reshape.235), calls=%async_computation.2 | async-start | bytes 262144 | tf_op jit(solution)/shard_map/all_to_all | solution.py:105
  299.5 218.8 %all-reduce.6.cloned.1.call-start = ((), (), s32[]{:S(2)}) async-start(), calls=%async_computation.6 | async-start | bytes 1769472 | tf_op jit(solution)/shard_map/psum | solution.py:112
  302.7 2.9 copy-start.2
  343.0 1.6 copy-start.5
  346.3 1.7 copy-start.4
  348.0 1.4 copy-start.10
  351.5 1.2 copy-start.7
  351.5 1.3 copy-start.17
  358.1 1.2 copy-start.11
  364.8 1.0 copy-start.15
  369.1 0.9 copy-start.12
  370.0 204.1 %all-gather.5.cloned.1.call-start = ((), (), s32[]{:S(2)}) async-start(), calls=%async_computation.5 | async-start | bytes 3760128 | tf_op jit(solution)/shard_map/all_gather | solution.py:106
  518.3 59.2 %copy-start.1 = (bf16[3,3,3,128,256]{4,3,2,1,0:T(8,128)(2,1)S(1)}, bf16[3,3,3,128,256]{4,3,2,1,0:T(8,128)(2,1)}, u32[]{:S(2)}) copy-start(bf16[3,3,3,128,256]{4,3,2,1,0:T(8,128)(2,1)} %param.8) | copy-start | bytes 5308420
  (1 other events, 0.7 us)
Sparse Core Ops, SparseCore 0:
  115.0 93.9 reduce-scatter.1
  211.3 52.0 all-gather.2
  370.1 148.1 all-reduce.5
  521.5 52.6 all-gather.4
